TPU v7x, 32 devices: a whole 2x2x4 slice. The times are simulated.
32 devices in a mesh: groups: 2 (over y), seq: 4 (over z), mp: 2 (over x), batch: 2 (over core).
Axes of the slice: x: 2, y: 2, z: 4, core: 2. Of those that a mesh axis runs over, the one named last changes fastest.
Arguments:
- hidden: bfloat16 [4, 1024, 2048], P(('groups', 'batch'), 'seq', 'mp'), parts along dimension 0, may hold values from -6 to 6
- segment_ids: int32 [4, 1024], P(('groups', 'batch'), 'seq'), parts along dimension 0, may hold values from 0 to 3, never falling along the last dimension, each value on 1 to 512 neighbouring positions
- norm_gain: float32 [2048], replicated, may hold values from 0.1 to 1.9
- w_gate: bfloat16 [2048, 2048], P('seq', 'mp'), may hold values from -0.125 to 0.125
- w_value: bfloat16 [2048, 2048], P('seq', 'mp'), may hold values from -0.125 to 0.125
- w_in_out: bfloat16 [2048, 256], P('seq', 'mp'), may hold values from -0.125 to 0.125
- w_step: bfloat16 [2048, 32], P('seq', 'mp'), may hold values from -0.125 to 0.125
- step_bias: float32 [32], P('mp'), may hold values from -3 to -1
- decay_rate: float32 [32], P('mp'), may hold values from 0 to 1, as said below
- skip_gain: float32 [32], P('mp'), may hold values from 0.5 to 1.5
- conv_value: bfloat16 [4, 2048], P(None, 'mp'), may hold values from -3 to 3
- conv_in_out: bfloat16 [4, 256], P(None, 'mp'), may hold values from -3 to 3
- w_out: bfloat16 [2048, 2048], P('mp', 'seq'), may hold values from -0.125 to 0.125
Outputs:
- mixed_out: bfloat16 [4, 1024, 2048], P(('groups', 'batch'), 'seq', 'mp'), parts along dimension 0
There are 2 independent parts, one for each index of `groups`. A program takes and returns all parts, laid end to end along the dimension named above; an argument that names none is the same for every part. Nothing has to cross between parts.
Inputs may be any that keep to these rules, and one draw needn't show every extreme that they name: `decay_rate`: each head's rate is positive and at most 0.15.
All inputs are finite; a program needn't handle non-finite values.
Results may differ from a plain program's by a relative error of at most 0.0076.
Values may be sent and summed in bfloat16 or wider, within the bound.
A program may use at most 64 MiB of HBM per device.

v0:
```python
import jax
import jax.numpy as jnp
from jax import lax
from jax.sharding import PartitionSpec as P

SPAN = 256
GROUP_HEADS = 8


def with_halo(block, sides, width):
    for axis, dim in sides:
        count = lax.axis_size(axis)
        forward = [(i, i + 1) for i in range(count - 1)]
        backward = [(target, source) for source, target in forward]
        low = lax.ppermute(
            lax.slice_in_dim(block, block.shape[dim] - width, None, axis=dim), axis, forward
        )
        high = lax.ppermute(lax.slice_in_dim(block, 0, width, axis=dim), axis, backward)
        block = jnp.concatenate([low, block, high], axis=dim)
    return block


def passed_along(value, axis, by):
    size = lax.axis_size(axis)
    pairs = [(i, i + by) for i in range(size) if 0 <= i + by < size]
    return lax.ppermute(value, axis, pairs)


def entering(value, axis, combine, identity, reverse):
    size, index = (lax.axis_size(axis), lax.axis_index(axis))
    everything = jax.tree.map(
        lambda part, kind: lax.all_gather(part.astype(kind), axis),
        value,
        (jnp.bfloat16, jnp.bfloat16),
    )
    start = jax.tree.map(
        lambda part, zero: jnp.broadcast_to(jnp.asarray(zero, part.dtype), part.shape),
        value,
        identity,
    )

    def lap(k, before):
        at = size - 1 - k if reverse else k
        reached = at > index if reverse else at < index
        new = combine(
            before, jax.tree.map(lambda part, own: part[at].astype(own.dtype), everything, value)
        )
        return jax.tree.map(lambda a, b: jnp.where(reached, a, b), new, before)

    return lax.fori_loop(0, size, lap, start)


def span_terms(values, input_maps, output_maps, log_decay, step_size, segment, segment_before):
    span_rows = values.shape[0]
    cumulative = jnp.cumsum(log_decay, axis=0)
    scores = jnp.dot(output_maps, input_maps.T, preferred_element_type=jnp.float32)
    row_index = lax.broadcasted_iota(jnp.int32, (span_rows, span_rows), 0)
    col_index = lax.broadcasted_iota(jnp.int32, (span_rows, span_rows), 1)
    allowed = (segment[:, None] == segment[None, :]) & (col_index <= row_index)
    cum_heads = cumulative.T
    spread = cum_heads[:, :, None] - cum_heads[:, None, :]
    weights = jnp.where(allowed[None], jnp.exp(jnp.where(allowed[None], spread, 0.0)), 0.0)
    mixing = (scores[None] * weights * step_size.T[:, None, :]).astype(jnp.bfloat16)
    intra_part = jnp.einsum("hij,jhp->ihp", mixing, values, preferred_element_type=jnp.float32)
    final_cum = cumulative[-1]
    same_end = (segment == segment[-1]).astype(jnp.float32)
    to_end = jnp.exp(final_cum[None] - cumulative) * step_size * same_end[:, None]
    weighted = (values.astype(jnp.float32) * to_end[:, :, None]).astype(jnp.bfloat16)
    span_state = jnp.einsum("jhp,jn->hpn", weighted, input_maps, preferred_element_type=jnp.float32)
    inflow = jnp.exp(cumulative) * (segment == segment_before).astype(jnp.float32)[:, None]
    passing = jnp.exp(final_cum) * (segment[-1] == segment_before).astype(jnp.float32)
    return (intra_part, span_state, inflow, passing)


def causal_conv(series, prior_rows, kernel):
    length_rows = series.shape[1]
    padded = jnp.concatenate([prior_rows, series], 1).astype(jnp.float32)
    summed = jnp.zeros(series.shape, jnp.float32)
    for tap_index in range(kernel.shape[0]):
        summed = (
            summed
            + kernel[tap_index].astype(jnp.float32) * padded[:, tap_index : tap_index + length_rows]
        )
    return jax.nn.silu(summed).astype(jnp.bfloat16)


def normalize(block_rows):
    widened = block_rows.astype(jnp.float32)
    return widened * lax.rsqrt(jnp.mean(widened * widened, axis=1, keepdims=True) + 1e-05)


def combine(earlier_part, later_part):
    return (
        earlier_part[0] * later_part[0],
        later_part[0][..., None, None] * earlier_part[1] + later_part[1],
    )


def compose(carried, inputs_pair):
    state_now, decay_now = carried
    span_state, span_pass = inputs_pair
    return (
        (span_pass[..., None, None] * state_now + span_state, decay_now * span_pass),
        (state_now, decay_now),
    )


def body(
    hidden,
    segment_ids,
    norm_gain,
    w_gate,
    w_value,
    w_in_out,
    w_step,
    step_bias,
    decay_rate,
    skip_gain,
    conv_value,
    conv_in_out,
    w_out,
):
    rows_local = hidden[0]
    segment = segment_ids[0]
    tok_count = rows_local.shape[0]
    extended = with_halo(segment, (("seq", 0),), 1)
    forward_full = lax.all_gather(rows_local, "mp", axis=1, tiled=True)
    reverse_full = forward_full[::-1]
    reverse_edges = extended[::-1]
    forward_in = (normalize(forward_full) * norm_gain).astype(jnp.bfloat16)
    reverse_in = (normalize(reverse_full)[:, ::-1] * norm_gain).astype(jnp.bfloat16)
    both_in = jnp.concatenate([forward_in, reverse_in], 0)
    pieces = (
        lax.all_gather(w_gate, "seq", axis=0, tiled=True),
        lax.all_gather(w_value, "seq", axis=0, tiled=True),
        lax.all_gather(w_in_out, "seq", axis=0, tiled=True),
        lax.all_gather(w_step, "seq", axis=0, tiled=True),
    )
    gate_sum, value_sum, inout_sum, step_sum = tuple(
        (jnp.dot(both_in, weight, preferred_element_type=jnp.float32) for weight in pieces)
    )
    gate_all = gate_sum.astype(jnp.bfloat16).reshape(2, tok_count, -1)
    value_pre = value_sum.astype(jnp.bfloat16).reshape(2, tok_count, -1)
    inout_pre = inout_sum.astype(jnp.bfloat16).reshape(2, tok_count, -1)
    reach_rows = conv_value.shape[0] - 1
    value_tail = value_pre[:, tok_count - reach_rows :]
    inout_tail = inout_pre[:, tok_count - reach_rows :]
    forward_prior = passed_along((value_tail[0], inout_tail[0]), "seq", 1)
    reverse_prior = passed_along((value_tail[1], inout_tail[1]), "seq", -1)
    value_prior = jnp.stack([forward_prior[0], reverse_prior[0]])
    inout_prior = jnp.stack([forward_prior[1], reverse_prior[1]])
    values_conv = causal_conv(value_pre, value_prior, conv_value)
    inout_conv = causal_conv(inout_pre, inout_prior, conv_in_out)
    inout_full = lax.all_gather(inout_conv, "mp", axis=2, tiled=True)
    state_width = inout_full.shape[2] // 2
    step_size = jax.nn.softplus(step_sum.reshape(2, tok_count, -1) + step_bias)
    log_decay = -step_size * decay_rate
    heads_local = step_size.shape[2]
    head_width = values_conv.shape[2] // heads_local
    count_spans = tok_count // SPAN
    segments_pair = jnp.stack([extended[1:-1], reverse_edges[1:-1]]).reshape(2, count_spans, SPAN)
    priors_pair = jnp.stack([extended[0], reverse_edges[0]])
    before_pair = jnp.concatenate([priors_pair[:, None], segments_pair[:, :-1, -1]], 1)
    span_values = values_conv.reshape(2, count_spans, SPAN, heads_local, head_width)
    span_inputs = inout_full[..., :state_width].reshape(2, count_spans, SPAN, state_width)
    span_outputs = inout_full[..., state_width:].reshape(2, count_spans, SPAN, state_width)
    span_logs = log_decay.reshape(2, count_spans, SPAN, heads_local)
    span_steps = step_size.reshape(2, count_spans, SPAN, heads_local)
    intra_part, states, inflow, passing = jax.vmap(jax.vmap(span_terms))(
        span_values, span_inputs, span_outputs, span_logs, span_steps, segments_pair, before_pair
    )
    start_pair = (
        jnp.zeros(states.shape[:1] + states.shape[2:], jnp.float32),
        jnp.ones((2, heads_local), jnp.float32),
    )
    summary_pair, before_parts = lax.scan(
        compose, start_pair, (jnp.moveaxis(states, 1, 0), jnp.moveaxis(passing, 1, 0))
    )
    summary_state, summary_decay = summary_pair
    before_states, before_decay = before_parts
    identity = (jnp.ones_like(summary_decay[0]), jnp.zeros_like(summary_state[0]))
    forward_entry = entering((summary_decay[0], summary_state[0]), "seq", combine, identity, False)
    reverse_entry = entering((summary_decay[1], summary_state[1]), "seq", combine, identity, True)
    entry_state = jnp.stack([forward_entry[1], reverse_entry[1]])
    span_entry = before_states + before_decay[..., None, None] * entry_state[None]
    span_entry = jnp.moveaxis(span_entry, 0, 1).astype(jnp.bfloat16)
    carried = jnp.einsum(
        "skin,skhpn->skihp", span_outputs, span_entry, preferred_element_type=jnp.float32
    )
    mixed = (
        intra_part
        + inflow[..., None] * carried
        + skip_gain[:, None] * span_values.astype(jnp.float32)
    )
    mixed = mixed.reshape(2, tok_count, heads_local * head_width)
    gate_wide = lax.optimization_barrier(gate_all).astype(jnp.float32)
    gated_out = mixed * jax.nn.silu(gate_wide)
    grouped = gated_out.reshape(2, tok_count, -1, GROUP_HEADS * head_width)
    normed = grouped * lax.rsqrt(jnp.mean(grouped * grouped, axis=3, keepdims=True) + 1e-05)
    normed = normed.reshape(2, tok_count, heads_local * head_width).astype(jnp.bfloat16)
    forward_mix = normed[0]
    reverse_mix = normed[1][::-1]
    block_cols = lax.all_gather(w_out, "seq", axis=1, tiled=True)
    direct = jnp.dot(forward_mix, block_cols, preferred_element_type=jnp.float32)
    flipped = jnp.dot(reverse_mix, block_cols, preferred_element_type=jnp.float32)[:, ::-1]
    running = direct
    running = running + flipped
    result = lax.psum_scatter(running, "mp", scatter_dimension=1, tiled=True).astype(jnp.bfloat16)
    return result[None]


def solution(mesh):
    placed = (
        P(("groups", "batch"), "seq", "mp"),
        P(("groups", "batch"), "seq"),
        P(),
        P("seq", "mp"),
        P("seq", "mp"),
        P("seq", "mp"),
        P("seq", "mp"),
        P("mp"),
        P("mp"),
        P("mp"),
        P(None, "mp"),
        P(None, "mp"),
        P("mp", "seq"),
    )
    return jax.shard_map(
        body,
        mesh=mesh,
        in_specs=placed,
        out_specs=P(("groups", "batch"), "seq", "mp"),
        check_vma=False,
    )
```

profile of v0, /device:TPU:0, one launch (start us, length us, event | category | flops | bytes accessed | tf_op | source)
XLA Modules:
  0.0 399.6 jit_solution(7486551002777506659)
XLA Ops:
  9.3 5.4 %collective-permute-start.4 = (s32[1]{0:T(128)}, s32[1]{0:T(128)}, u32[]{:S(2)}, u32[]{:S(2)}) collective-permute-start(s32[1]{0:T(128)} %bitcast.30), channel_id=1, source_target_pairs={{0,4},{4,8},{8,12},{1,5},{5,9},{9,13},{2,6},{6,10},{10,14},{3,7},{... | collective-permute-start | bytes 20 | tf_op jit(solution)/shard_map/ppermute | solution.py:15
  16.1 14.1 %all_gather.41 = bf16[2048,16]{0,1:T(8,128)(2,1)S(1)} all-gather(bf16[512,16]{0,1:T(8,128)(2,1)S(1)} %copy-done.17), channel_id=1, replica_groups=mesh['groups'=2,'seq'=4,'mp'=2,'batch'=2] {'seq'}, dimensions={0}, use_global_device_ids=true | all-gather | bytes 81920 | tf_op jit(solution)/shard_map/all_gather | solution.py:137
  30.5 17.5 %all_gather.39 = bf16[2048,128]{1,0:T(8,128)(2,1)} all-gather(bf16[512,128]{1,0:T(8,128)(2,1)S(1)} %copy-done.12), channel_id=1, replica_groups=mesh['groups'=2,'seq'=4,'mp'=2,'batch'=2] {'seq'}, dimensions={0}, use_global_device_ids=true | all-gather | bytes 655360 | tf_op jit(solution)/shard_map/all_gather | solution.py:136
  50.8 12.6 %rev.13 = bf16[256,2048]{1,0:T(8,128)(2,1)S(1)} reverse(bf16[256,2048]{1,0:T(8,128)(2,1)} %bitcast.139), dimensions={0} | reverse | bytes 2097152 | tf_op jit(solution)/shard_map/rev | solution.py:128
  65.3 15.0 %rev.14 = f32[256,2048]{1,0:T(8,128)S(1)} reverse(f32[256,2048]{1,0:T(8,128)} %convert_multiply_fusion.1), dimensions={1} | reverse | bytes 4194304 | tf_op jit(solution)/shard_map/rev | solution.py:131
  85.1 2.4 convolution_convert_fusion.2
  87.5 4.0 collective-permute-start.2
  94.4 3.9 collective-permute-done.3
  98.5 16.9 %all-gather.10.cloned.1.call-done = bf16[2048,1024]{1,0:T(8,128)(2,1)} async-done(((bf16[512,1024]{1,0:T(8,128)(2,1)}), bf16[2048,1024]{1,0:T(8,128)(2,1)}) %all-gather.10.cloned.1.call-update) | async-done | bytes 4194320 | tf_op jit(solution)/shard_map/all_gather | solution.py:135
  115.4 4.5 %convolution_convert_fusion.1 = bf16[512,1024]{1,0:T(8,128)(2,1)S(1)} fusion(bf16[2048,1024]{1,0:T(8,128)(2,1)} %all-gather.10.cloned.1.call-done, bf16[256,2048]{1,0:T(8,128)(2,1)S(1)} %copy-done.9, bf16[256,2048]{1,0:T(8,128)(2,1)S(1)} %copy-done.7), kind=kOutput, calls=%fused_computation.44 | convolution fusion | flops 2152202240 | bytes 7340032 | tf_op jit(solution)/shard_map/dot_general | solution.py:140
  119.9 2.1 collective-permute-start
  123.3 5.8 %all_gather.40 = bf16[2,256,256]{2,1,0:T(8,128)(2,1)S(1)} all-gather(bf16[2,256,128]{2,1,0:T(8,128)(2,1)S(1)} %multiply_convert_fusion.9), channel_id=1, replica_groups=mesh['groups'=2,'seq'=4,'mp'=2,'batch'=2] {'mp'}, dimensions={2}, use_global_device_ids=true | all-gather | bytes 393216 | tf_op jit(solution)/shard_map/all_gather | solution.py:154
  134.1 11.3 %all-gather.1 = bf16[4,1,16]{2,1,0:T(2,128)(2,1)S(1)} all-gather(bf16[1,1,16]{2,1,0:T(2,128)(2,1)S(1)} %get-tuple-element.338), channel_id=3, replica_groups=mesh['groups'=2,'seq'=4,'mp'=2,'batch'=2] {'seq'}, dimensions={0}, use_global_device_ids=true | all-gather | bytes 160 | tf_op jit(solution)/shard_map/all_gather | solution.py:32
  145.5 8.4 %all-gather.2 = bf16[4,1,16]{2,1,0:T(2,128)(2,1)S(1)} all-gather(bf16[1,1,16]{2,1,0:T(2,128)(2,1)S(1)} %get-tuple-element.339), channel_id=4, replica_groups=mesh['groups'=2,'seq'=4,'mp'=2,'batch'=2] {'seq'}, dimensions={0}, use_global_device_ids=true | all-gather | bytes 160 | tf_op jit(solution)/shard_map/all_gather | solution.py:32
  155.6 41.3 %all-gather.16.cloned.1.call-done = bf16[2048,1024]{1,0:T(8,128)(2,1)} async-done(((bf16[512,1024]{1,0:T(8,128)(2,1)}), bf16[2048,1024]{1,0:T(8,128)(2,1)}) %all-gather.16.cloned.1.call-update) | async-done | bytes 4194320 | tf_op jit(solution)/shard_map/all_gather | solution.py:134
  196.9 5.2 %convolution_convert_fusion = bf16[512,1024]{1,0:T(8,128)(2,1)S(1)} fusion(bf16[2048,1024]{1,0:T(8,128)(2,1)} %all-gather.16.cloned.1.call-done, bf16[256,2048]{1,0:T(8,128)(2,1)} %copy-done.8, bf16[256,2048]{1,0:T(8,128)(2,1)} %copy-done.6), kind=kOutput, calls=%fused_computation.43 | convolution fusion | flops 2152202240 | bytes 7340032 | tf_op jit(solution)/shard_map/dot_general | solution.py:140
  203.7 21.1 %all-gather.12.cloned.1.call-done = bf16[4,16,64,128]{3,2,1,0:T(8,128)(2,1)} async-done(((bf16[1,16,64,128]{3,2,1,0:T(8,128)(2,1)}), bf16[4,16,64,128]{3,2,1,0:T(8,128)(2,1)}) %all-gather.12.cloned.1.call-update) | async-done | bytes 1048592 | tf_op jit(solution)/shard_map/all_gather | solution.py:32
  224.8 4.5 %while.37 = (s32[]{:T(128)}, f32[16,64,128]{2,1,0:T(8,128)S(1)}, s32[]{:T(128)}, bf16[4,16]{1,0:T(4,128)(2,1)S(1)}, bf16[4,16,64,128]{3,2,1,0:T(8,128)(2,1)}, /*index=5*/s32[]{:T(128)}, s32[]{:T(128)}) while((s32[]{:T(128)}, f32[16,64,128]{2,1,0:T(8,128)S(1)}, s32[]{:T(128)}, bf16[4,16]{1,0:T(4,128)(2,1)S(1)}, ...), condition=%wide.region_5.6_spmd.clone, body=%wide.region_4.5_spmd.clone.sunk | while | flops 655380 | bytes 1310985 | solution.py:50
  229.3 24.4 %all-gather.14.cloned.1.call-done = bf16[4,16,64,128]{3,2,1,0:T(8,128)(2,1)} async-done(((bf16[1,16,64,128]{3,2,1,0:T(8,128)(2,1)}), bf16[4,16,64,128]{3,2,1,0:T(8,128)(2,1)}) %all-gather.14.cloned.1.call-update) | async-done | bytes 1048592 | tf_op jit(solution)/shard_map/all_gather | solution.py:32
  253.7 4.5 %while.38 = (s32[]{:T(128)}, f32[16,64,128]{2,1,0:T(8,128)S(1)}, s32[]{:T(128)}, bf16[4,16]{1,0:T(4,128)(2,1)S(1)}, bf16[4,16,64,128]{3,2,1,0:T(8,128)(2,1)}, /*index=5*/s32[]{:T(128)}, s32[]{:T(128)}, s32[]{:T(128)}, s32[]{:T(128)}) while((s32[]{:T(128)}, f32[16,64,128]{2,1,0:T(8,128)S(1)}, s32[]{:T(128)}, ...), condition=%wide.region_7.8_spmd.clone, body=%wide.region_6.7_spmd.clone.sunk | while | flops 655384 | bytes 1311047 | solution.py:50
  260.2 4.3 %fusion.20 = f32[2,1,256,16,64]{2,4,3,0,1:T(8,128)} fusion(f32[2,1,256,16,64]{2,4,3,0,1:T(8,128)S(1)} %bitcast.142, f32[2,256,16,64]{1,3,2,0:T(8,128)S(1)} %fusion.23, bf16[2,256,16,64]{1,3,2,0:T(8,128)(2,1)S(1)} %bitcast.147, f32[2,16,256]{2,1,0:T(8,128)S(1)} %copy-done.16, f32[2,16,256]{2,1,0:T(8,128)S(1)} %copy-done.13, ...), kind=kOutput, calls=%fused_computation.38 | convolution fusion | flops 283115520 | bytes 8093760 | tf_op jit(solution)/shard_map/vmap(vmap(hij,jhp->ihp))/dot_general | solution.py:64
  264.5 2.0 copy.95
  268.4 4.1 %mul.393 = f32[2,256,2,512]{3,2,1,0:T(2,128)} reshape(f32[2,256,1024]{2,1,0:T(8,128)} %fusion.45) | data formatting | bytes 4194304 | tf_op jit(solution)/shard_map/mul | solution.py:199
  272.5 2.2 reduce_sum.29
  276.6 4.1 %mul.395 = f32[2,256,1024]{2,1,0:T(8,128)} reshape(f32[2,256,2,512]{3,2,1,0:T(2,128)} %mul.394) | data formatting | bytes 4194304 | tf_op jit(solution)/shard_map/mul | solution.py:199
  280.7 2.4 multiply_convert_fusion.2
  284.7 50.7 %all-gather.18.cloned.1.call-done = bf16[1024,2048]{1,0:T(8,128)(2,1)} async-done(((bf16[1024,512]{1,0:T(8,128)(2,1)}), bf16[1024,2048]{1,0:T(8,128)(2,1)}) %all-gather.18.cloned.1.call-update) | async-done | bytes 4194320 | tf_op jit(solution)/shard_map/all_gather | solution.py:203
  335.4 4.8 %fusion.49 = f32[256,2048]{1,0:T(8,128)} fusion(bf16[256,1024]{1,0:T(8,128)(2,1)S(1)} %rev.15, bf16[1024,2048]{1,0:T(8,128)(2,1)} %all-gather.18.cloned.1.call-done), kind=kOutput, calls=%fused_computation.125 | convolution fusion | flops 1073741824 | bytes 6815744 | tf_op jit(solution)/shard_map/dot_general | solution.py:205
  340.2 15.0 %rev.16 = f32[256,2048]{1,0:T(8,128)S(1)} reverse(f32[256,2048]{1,0:T(8,128)} %fusion.49), dimensions={1} | reverse | bytes 4194304 | tf_op jit(solution)/shard_map/rev | solution.py:205
  355.2 4.8 %convolution_add_fusion = f32[256,2048]{1,0:T(8,128)} fusion(f32[256,2048]{1,0:T(8,128)S(1)} %rev.16, bf16[1024,2048]{1,0:T(8,128)(2,1)} %all-gather.18.cloned.1.call-done, bf16[2,256,1024]{2,1,0:T(8,128)(2,1)S(1)} %copy-done.2), kind=kOutput, calls=%fused_computation.20 | convolution fusion | flops 1074266112 | bytes 8912896 | tf_op jit(solution)/shard_map/dot_general | solution.py:204
  360.1 30.5 %reduce-scatter.2.cloned.1.call-done = f32[256,1024]{1,0:T(8,128)} async-done(((f32[256,2048]{1,0:T(8,128)}), f32[256,1024]{1,0:T(8,128)}) %reduce-scatter.2.cloned.1.call-update) | async-done | bytes 1048592 | tf_op jit(solution)/shard_map/reduce_scatter | solution.py:208
  390.6 2.1 convert_bitcast_fusion
  (149 shorter events, 42.4 us)
Async XLA Ops:
  6.5 23.6 %copy-start.18 = (s32[1,256]{1,0:T(1,128)S(1)}, s32[1,256]{1,0:T(1,128)}, u32[]{:S(2)}) copy-start(s32[1,256]{1,0:T(1,128)} %param.18) | copy-start | bytes 3076
  6.5 9.6 %copy-start.17 = (bf16[512,16]{0,1:T(8,128)(2,1)S(1)}, bf16[512,16]{0,1:T(8,128)(2,1)}, u32[]{:S(2)}) copy-start(bf16[512,16]{0,1:T(8,128)(2,1)} %param.23) | copy-start | bytes 49156
  6.5 23.9 %copy-start.12 = (bf16[512,128]{1,0:T(8,128)(2,1)S(1)}, bf16[512,128]{1,0:T(8,128)(2,1)}, u32[]{:S(2)}) copy-start(bf16[512,128]{1,0:T(8,128)(2,1)} %param.22) | copy-start | bytes 393220
  6.5 41.5 %copy-start.20 = (bf16[4,128]{1,0:T(4,128)(2,1)S(1)}, bf16[4,128]{1,0:T(4,128)(2,1)}, u32[]{:S(2)}) copy-start(bf16[4,128]{1,0:T(4,128)(2,1)} %param.28) | copy-start | bytes 3076
  6.5 41.5 %copy-start.14 = (bf16[4,1024]{1,0:T(4,128)(2,1)S(1)}, bf16[4,1024]{1,0:T(4,128)(2,1)}, u32[]{:S(2)}) copy-start(bf16[4,1024]{1,0:T(4,128)(2,1)} %param.27) | copy-start | bytes 24580
  6.5 44.2 %all-gather.20.cloned.1.call-start = ((), (), s32[]{:S(2)}) async-start(), calls=%async_computation.7 | async-start | bytes 1572864 | tf_op jit(solution)/shard_map/all_gather | solution.py:127
  7.3 108.1 %all-gather.10.cloned.1.call-start = ((), (), s32[]{:S(2)}) async-start(), calls=%async_computation.1 | async-start | bytes 5242880 | tf_op jit(solution)/shard_map/all_gather | solution.py:135
  8.0 188.9 %all-gather.16.cloned.1.call-start = ((), (), s32[]{:S(2)}) async-start(), calls=%async_computation.4 | async-start | bytes 5242880 | tf_op jit(solution)/shard_map/all_gather | solution.py:134
  9.3 38.7 %collective-permute-start.4 = (s32[1]{0:T(128)}, s32[1]{0:T(128)}, u32[]{:S(2)}, u32[]{:S(2)}) collective-permute-start(s32[1]{0:T(128)} %bitcast.30), channel_id=1, source_target_pairs={{0,4},{4,8},{8,12},{1,5},{5,9},{9,13},{2,6},{6,10},{10,14},{3,7},{... | collective-permute-start | bytes 20 | tf_op jit(solution)/shard_map/ppermute | solution.py:15
  14.7 33.3 %collective-permute-start.5 = (s32[1]{0:T(128)}, s32[1]{0:T(128)}, u32[]{:S(2)}, u32[]{:S(2)}) collective-permute-start(s32[1]{0:T(128)} %bitcast.31), channel_id=1, source_target_pairs={{4,0},{8,4},{12,8},{5,1},{9,5},{13,9},{6,2},{10,6},{14,10},{7,3},{... | collective-permute-start | bytes 20 | tf_op jit(solution)/shard_map/ppermute | solution.py:18
  16.0 208.8 %all-gather.12.cloned.1.call-start = ((), (), s32[]{:S(2)}) async-start(), calls=%async_computation.2 | async-start | bytes 1310720 | tf_op jit(solution)/shard_map/all_gather | solution.py:32
  65.3 15.0 %copy-start = (bf16[1,256,2048]{2,1,0:T(8,128)(2,1)S(1)}, bf16[1,256,2048]{2,1,0:T(8,128)(2,1)}, u32[]{:S(2)}) copy-start(bf16[1,256,2048]{2,1,0:T(8,128)(2,1)} %all-gather.20.cloned.1.call-done) | copy-start | bytes 3145732
  65.3 15.3 %copy-start.19 = (f32[2048]{0:T(1024)S(1)}, f32[2048]{0:T(1024)}, u32[]{:S(2)}) copy-start(f32[2048]{0:T(1024)} %param.19) | copy-start | bytes 24580
  81.2 2.1 copy-start.21
  81.2 2.1 copy-start.22
  82.6 2.5 copy-start.10
  85.1 30.3 %copy-start.7 = (bf16[256,2048]{1,0:T(8,128)(2,1)S(1)}, bf16[256,2048]{1,0:T(8,128)(2,1)}, u32[]{:S(2)}) copy-start(bf16[256,2048]{1,0:T(8,128)(2,1)} %copy-done.6) | copy-start | bytes 3145732
  85.1 30.3 %copy-start.9 = (bf16[256,2048]{1,0:T(8,128)(2,1)S(1)}, bf16[256,2048]{1,0:T(8,128)(2,1)}, u32[]{:S(2)}) copy-start(bf16[256,2048]{1,0:T(8,128)(2,1)} %copy-done.8) | copy-start | bytes 3145732
  87.5 6.9 %collective-permute-start.2 = (bf16[3,128]{1,0:T(4,128)(2,1)S(1)}, bf16[3,128]{1,0:T(4,128)(2,1)S(1)}, u32[]{:S(2)}, u32[]{:S(2)}) collective-permute-start(bf16[3,128]{1,0:T(4,128)(2,1)S(1)} %get-tuple-element.318), channel_id=1, source_target_pairs={{0,4},{4,8},{8,12},{1,5},{5,9},{9,13},{2,6},{6,10},{10,14},{3,7},{... | collective-permute-start | bytes 2312 | tf_op jit(solution)/shard_map/ppermute | solution.py:26
  91.5 6.7 %collective-permute-start.3 = (bf16[3,128]{1,0:T(4,128)(2,1)S(1)}, bf16[3,128]{1,0:T(4,128)(2,1)S(1)}, u32[]{:S(2)}, u32[]{:S(2)}) collective-permute-start(bf16[3,128]{1,0:T(4,128)(2,1)S(1)} %get-tuple-element.319), channel_id=1, source_target_pairs={{4,0},{8,4},{12,8},{5,1},{9,5},{13,9},{6,2},{10,6},{14,10},{7,3},{... | collective-permute-start | bytes 2312 | tf_op jit(solution)/shard_map/ppermute | solution.py:26
  119.9 9.2 %collective-permute-start = (bf16[3,1024]{1,0:T(4,128)(2,1)S(1)}, bf16[3,1024]{1,0:T(4,128)(2,1)S(1)}, u32[]{:S(2)}, u32[]{:S(2)}) collective-permute-start(bf16[3,1024]{1,0:T(4,128)(2,1)S(1)} %get-tuple-element.314), channel_id=1, source_target_pairs={{0,4},{4,8},{8,12},{1,5},{5,9},{9,13},{2,6},{6,10},{10,14},{3,7},{... | collective-permute-start | bytes 18440 | tf_op jit(solution)/shard_map/ppermute | solution.py:26
  122.0 7.1 %collective-permute-start.1 = (bf16[3,1024]{1,0:T(4,128)(2,1)S(1)}, bf16[3,1024]{1,0:T(4,128)(2,1)S(1)}, u32[]{:S(2)}, u32[]{:S(2)}) collective-permute-start(bf16[3,1024]{1,0:T(4,128)(2,1)S(1)} %get-tuple-element.315), channel_id=1, source_target_pairs={{4,0},{8,4},{12,8},{5,1},{9,5},{13,9},{6,2},{10,6},{14,10},{7,3},{... | collective-permute-start | bytes 18440 | tf_op jit(solution)/shard_map/ppermute | solution.py:26
  131.2 2.5 copy-start.4
  132.6 121.1 %all-gather.14.cloned.1.call-start = ((), (), s32[]{:S(2)}) async-start(), calls=%async_computation.3 | async-start | bytes 1310720 | tf_op jit(solution)/shard_map/all_gather | solution.py:32
  133.1 202.3 %all-gather.18.cloned.1.call-start = ((), (), s32[]{:S(2)}) async-start(), calls=%async_computation.5 | async-start | bytes 5242880 | tf_op jit(solution)/shard_map/all_gather | solution.py:203
  133.7 256.9 %reduce-scatter.2.cloned.1.call-start = ((), (), s32[]{:S(2)}) async-start(), calls=%async_computation.6 | async-start | bytes 3145728 | tf_op jit(solution)/shard_map/reduce_scatter | solution.py:208
  258.2 2.0 copy-start.11
  258.3 2.0 copy-start.13
  258.3 2.0 copy-start.15
  258.3 1.9 copy-start.16
  258.3 1.9 copy-start.23
  340.2 15.0 %copy-start.2 = (bf16[2,256,1024]{2,1,0:T(8,128)(2,1)S(1)}, bf16[2,256,1024]{2,1,0:T(8,128)(2,1)}, u32[]{:S(2)}) copy-start(bf16[2,256,1024]{2,1,0:T(8,128)(2,1)} %copy-done.1) | copy-start | bytes 3145732
  (5 other events, 6.8 us)
Sparse Core Ops, SparseCore 0:
  8.9 23.9 all-gather.19
  34.5 80.8 all-gather.9
  117.0 79.8 all-gather.15
  198.3 26.4 all-gather.11
  226.2 27.4 all-gather.13
  255.1 80.2 all-gather.17
  360.2 30.3 reduce-scatter.1
where the time goes:
time: 403 us; the launch traced here: 400 us
  waiting for transfers between devices  191 us (47%)
  local copies, waits for them, and re-layouts  64.4 us (16%)
  blocking collectives  57.2 us (14%)
  matrix products  28.5 us (7%)
  other arithmetic  28.4 us (7%)
  starting transfers between devices  15.6 us (4%)
  between operations  14 us (3%)
    all_gather x1, waiting for transfers between devices, body(): block_cols = lax.all_gather(w_out, 'seq', axis=1, tiled=True)  50.7 us
    all_gather x2, waiting for transfers between devices, entering(): lax.all_gather(part.astype(kind), axis)  45.4 us
    all_gather x1, waiting for transfers between devices, body(): lax.all_gather(w_gate, 'seq', axis=0, tiled=True)  41.3 us
    reduce_scatter x1, waiting for transfers between devices, body(): lax.psum_scatter(running, 'mp', scatter_dimension=1, tiled=True)  30.5 us
    all_gather x2, blocking collectives, entering(): lax.all_gather(part.astype(kind), axis)  19.8 us
    all_gather x1, blocking collectives, body(): lax.all_gather(w_in_out, 'seq', axis=0, tiled=True)  17.5 us
    all_gather x1, waiting for transfers between devices, body(): lax.all_gather(w_value, 'seq', axis=0, tiled=True)  16.9 us
    rev x1, local copies, waits for them, and re-layouts, body(): normalize(reverse_full)[:, ::-1] * norm_gain  15 us
  transfers between devices with their start and end apart: 13, of which 7 were waited for; matrix products, arithmetic and copies ran while one was open for 23% of the time, Pallas kernels for 0%

commit v1 on v0

--- a/solution.py
+++ b/solution.py
@@ -1,6 +1,10 @@
+import functools
+
 import jax
 import jax.numpy as jnp
 from jax import lax
+from jax.experimental import pallas as pl
+from jax.experimental.pallas import tpu as pltpu
 from jax.sharding import PartitionSpec as P
 
 SPAN = 256
@@ -52,7 +56,8 @@
 
 def span_terms(values, input_maps, output_maps, log_decay, step_size, segment, segment_before):
     span_rows = values.shape[0]
-    cumulative = jnp.cumsum(log_decay, axis=0)
+    earlier = jnp.tril(jnp.ones((span_rows, span_rows), jnp.float32))
+    cumulative = jnp.dot(earlier, log_decay, precision=lax.Precision.HIGHEST)
     scores = jnp.dot(output_maps, input_maps.T, preferred_element_type=jnp.float32)
     row_index = lax.broadcasted_iota(jnp.int32, (span_rows, span_rows), 0)
     col_index = lax.broadcasted_iota(jnp.int32, (span_rows, span_rows), 1)
@@ -209,6 +214,648 @@
     return result[None]
 
 
+MESH = pl.DeviceIdType.MESH
+F32 = jnp.float32
+BF16 = jnp.bfloat16
+
+
+def mm(a, b):
+    return jnp.dot(a, b, preferred_element_type=F32)
+
+
+def parts(value, count):
+    out = []
+    for _ in range(count):
+        piece = value.astype(BF16)
+        out.append(piece)
+        value = value - piece.astype(F32)
+    return out
+
+
+def fused_kernel(
+    S,
+    heads,
+    hidden,
+    segs,
+    gain,
+    w_value,
+    w_small,
+    w_gate,
+    w_out,
+    bias,
+    rate,
+    skip,
+    conv,
+    out,
+    hbuf,
+    wv,
+    wg,
+    wo,
+    u,
+    pre,
+    step,
+    gate,
+    tsend,
+    trecv,
+    maps,
+    xb,
+    smask,
+    cs,
+    ct,
+    dtt,
+    seg_col,
+    state,
+    inflow,
+    ein,
+    eout,
+    mixed,
+    mix,
+    osend,
+    orecv,
+    lsem,
+    hsem,
+    zsend,
+    zrecv,
+    ysend,
+    yrecv,
+    csend,
+    crecv,
+    tsem,
+    msem,
+    esend,
+    erecv,
+    osem,
+):
+    g = lax.axis_index("groups")
+    s = lax.axis_index("seq")
+    m = lax.axis_index("mp")
+    b = lax.axis_index("batch")
+    mine, across = g * 2 + b, (1 - g) * 2 + b
+    rows = hidden.shape[0]
+    half = hidden.shape[1]
+    chan = w_value.shape[1]
+    depth = w_value.shape[0]
+    out_cols = w_out.shape[1]
+    to_y, to_core, to_mp = {"groups": 1 - g}, {"batch": 1 - b}, {"mp": 1 - m}
+
+    barrier = pltpu.get_barrier_semaphore()
+    for peer in (to_y, to_core, to_mp):
+        pl.semaphore_signal(barrier, inc=1, device_id=peer, device_id_type=MESH)
+
+    @pl.when(s > 0)
+    def _():
+        pl.semaphore_signal(barrier, inc=1, device_id={"seq": s - 1}, device_id_type=MESH)
+
+    @pl.when(s < S - 1)
+    def _():
+        pl.semaphore_signal(barrier, inc=1, device_id={"seq": s + 1}, device_id_type=MESH)
+
+    own_rows = pl.ds(pl.multiple_of(s * depth, depth), depth)
+    local = [
+        pltpu.make_async_copy(hidden, hbuf.at[m], lsem.at[0]),
+        pltpu.make_async_copy(w_value, wv.at[own_rows, pl.ds(0, chan)], lsem.at[1]),
+        pltpu.make_async_copy(w_small, wv.at[own_rows, pl.ds(chan, 256)], lsem.at[2]),
+        pltpu.make_async_copy(w_gate, wg.at[own_rows], lsem.at[3]),
+        pltpu.make_async_copy(w_out, wo.at[s], lsem.at[4]),
+    ]
+    for copy in local:
+        copy.start()
+
+    lone = jnp.where((s == 0) | (s == S - 1), 1, 0)
+    pl.semaphore_wait(barrier, 5 - lone)
+
+    def piece(w, t, quarter):
+        if w == 2:
+            size = w_out.shape[0] // 4
+            return wo.at[t, pl.ds(pl.multiple_of(quarter * size, size), size)]
+        size = depth // 4
+        start = pl.multiple_of(t * depth + quarter * size, size)
+        return (wv, wg)[w].at[pl.ds(start, size)]
+
+    def came(d, k):
+        return s - k if d == 0 else s + k
+
+    def comes(d, k):
+        return s >= k if d == 0 else s + k <= S - 1
+
+    def z_copy(w, d, k):
+        part = piece(w, came(d, k - 1), mine)
+        peer = {"seq": s + 1 if d == 0 else s - 1}
+        return pltpu.make_async_remote_copy(
+            part, part, zsend.at[w, d, k - 1], zrecv.at[w, d, k - 1], peer, MESH
+        )
+
+    def z_wait(w, d, k):
+        part = piece(w, came(d, k), mine)
+        peer = {"seq": s - 1 if d == 0 else s + 1}
+        pltpu.make_async_remote_copy(
+            part, part, zsend.at[w, d, k - 1], zrecv.at[w, d, k - 1], peer, MESH
+        ).wait_recv()
+
+    def sends(d, k):
+        held = comes(d, k - 1)
+        return held & (s < S - 1) if d == 0 else held & (s > 0)
+
+    def y_copy(w, d, k, quarter):
+        part = piece(w, came(d, k), quarter)
+        return pltpu.make_async_remote_copy(
+            part, part, ysend.at[w, d, k - 1], yrecv.at[w, d, k - 1], to_y, MESH
+        )
+
+    def c_copy(w, d, k, which, quarter):
+        part = piece(w, came(d, k), quarter)
+        return pltpu.make_async_remote_copy(
+            part, part, csend.at[w, d, k - 1, which], crecv.at[w, d, k - 1, which], to_core, MESH
+        )
+
+    def start_round(w, k):
+        for d in (0, 1):
+
+            @pl.when(sends(d, k))
+            def _():
+                z_copy(w, d, k).start()
+
+    def step_a(w, k):
+        for d in (0, 1):
+
+            @pl.when(comes(d, k))
+            def _():
+                z_wait(w, d, k)
+                if k < S - 1:
+
+                    @pl.when(sends(d, k + 1))
+                    def _():
+                        z_copy(w, d, k + 1).start()
+
+                y_copy(w, d, k, mine).start()
+                c_copy(w, d, k, 0, mine).start()
+
+    def step_b(w, k):
+        for d in (0, 1):
+
+            @pl.when(comes(d, k))
+            def _():
+                y_copy(w, d, k, across).wait_recv()
+                c_copy(w, d, k, 1, across).start()
+
+    def step_c(w):
+        other = g * 2 + 1 - b
+        other_across = (1 - g) * 2 + 1 - b
+        for k in range(1, S):
+            for d in (0, 1):
+
+                @pl.when(comes(d, k))
+                def _():
+                    c_copy(w, d, k, 0, other).wait_recv()
+                    c_copy(w, d, k, 1, other_across).wait_recv()
+
+    def settle():
+        for w in range(3):
+            for k in range(1, S):
+                for d in (0, 1):
+
+                    @pl.when(sends(d, k))
+                    def _():
+                        z_copy(w, d, k).wait_send()
+
+                    @pl.when(comes(d, k))
+                    def _():
+                        y_copy(w, d, k, mine).wait_send()
+                        c_copy(w, d, k, 0, mine).wait_send()
+                        c_copy(w, d, k, 1, across).wait_send()
+
+    local[1].wait()
+    local[2].wait()
+    start_round(0, 1)
+    local[0].wait()
+    h_copy = pltpu.make_async_remote_copy(
+        hbuf.at[m], hbuf.at[m], hsem.at[0], hsem.at[1], to_mp, MESH
+    )
+    h_copy.start()
+    local[3].wait()
+    start_round(1, 1)
+    local[4].wait()
+
+    ri = lax.broadcasted_iota(jnp.int32, (rows, rows), 0)
+    ci = lax.broadcasted_iota(jnp.int32, (rows, rows), 1)
+    eye = ri == ci
+    anti = ri + ci == rows - 1
+    flip = jnp.where(anti, 1.0, 0.0).astype(BF16)
+    lower = jnp.where(ci <= ri, 1.0, 0.0).astype(BF16)
+
+    def turned(row, where):
+        return jnp.sum(jnp.where(where, row, 0.0), axis=1, keepdims=True)
+
+    seg_row = segs[...].astype(F32)
+    seg_c = turned(seg_row, eye)
+    seg_c_rev = turned(seg_row, anti)
+    seg_row_rev = jnp.sum(jnp.where(anti, seg_c, 0.0), axis=0, keepdims=True)
+    strand_rows = (seg_row, seg_row_rev)
+    strand_cols = (seg_c, seg_c_rev)
+    for st in (0, 1):
+        seg_col[st] = jnp.broadcast_to(strand_cols[st], (rows, 128))
+
+    step_a(0, 1)
+    step_a(1, 1)
+    step_b(0, 1)
+    pltpu.make_async_remote_copy(
+        hbuf.at[1 - m], hbuf.at[1 - m], hsem.at[0], hsem.at[1], to_mp, MESH
+    ).wait_recv()
+
+    total = jnp.zeros((rows, 1), F32)
+    for i in range(2):
+        wide = hbuf[i].astype(F32)
+        total = total + jnp.sum(wide * wide, axis=1, keepdims=True)
+    inv = lax.rsqrt(total / (2 * half) + 1e-05)
+    inv_row = jnp.sum(jnp.where(eye, inv, 0.0), axis=0, keepdims=True)
+    inv_rev = turned(inv_row, anti)
+    blocks = half // 256
+    for i in range(2 * blocks):
+        there = pl.ds(i * 256, 256)
+        back = pl.ds((2 * blocks - 1 - i) * 256, 256)
+        block = hbuf[i // blocks, :, (i % blocks) * 256 : (i % blocks + 1) * 256]
+        u[0:rows, there] = ((block.astype(F32) * inv) * gain[:, there]).astype(BF16)
+        turned_block = mm(mm(flip, block).astype(BF16), flip)
+        u[rows : 2 * rows, back] = ((turned_block * inv_rev) * gain[:, back]).astype(BF16)
+
+    step_a(0, 2)
+    step_b(1, 1)
+    step_a(1, 2)
+    step_b(0, 2)
+    step_a(0, 3)
+    start_round(2, 1)
+    step_b(1, 2)
+    step_b(0, 3)
+    step_c(0)
+
+    small = mm(u[...], wv[:, chan : chan + 256])
+    for st in (0, 1):
+        pre[st, 8 : 8 + rows, chan : chan + 128] = (
+            small[st * rows : (st + 1) * rows, :128].astype(BF16).astype(F32)
+        )
+        step[st] = small[st * rows : (st + 1) * rows, 128:]
+
+    @pl.loop(0, chan // 256)
+    def _(n):
+        cols = pl.ds(pl.multiple_of(n * 256, 256), 256)
+        got = mm(u[...], wv[:, cols]).astype(BF16).astype(F32)
+        for st in (0, 1):
+            pre[st, 8 : 8 + rows, cols] = got[st * rows : (st + 1) * rows]
+
+    def has_next(st):
+        return s < S - 1 if st == 0 else s > 0
+
+    def has_prev(st):
+        return s > 0 if st == 0 else s < S - 1
+
+    def t_copy(st):
+        peer = {"seq": s + 1 if st == 0 else s - 1}
+        return pltpu.make_async_remote_copy(
+            tsend.at[st], trecv.at[st], tsem.at[0, st], tsem.at[1, st], peer, MESH
+        )
+
+    for st in (0, 1):
+        tsend[st, :, 0 : chan + 128] = pre[st, rows - 8 : rows + 8, :].astype(BF16)
+        tsend[st, :, chan + 128 : chan + 256] = seg_col[st, rows - 16 : rows, :].astype(BF16)
+
+        @pl.when(has_next(st))
+        def _():
+            t_copy(st).start()
+
+    step_a(2, 1)
+    step_a(1, 3)
+    for st in (0, 1):
+        raw = step[st] + bias[...]
+        dt = jnp.maximum(raw, 0.0) + jnp.log1p(jnp.exp(-jnp.abs(raw)))
+        decay = -dt * rate[...]
+        c = sum(mm(lower, p) for p in parts(decay, 3))
+        cs[st] = c
+        ct[st] = c.T
+        dtt[st] = dt.T
+        last = c[rows - 1 : rows, :]
+        end = strand_cols[st][rows - 1 : rows, :]
+        step[st] = jnp.exp(last - c) * dt * jnp.where(strand_cols[st] == end, 1.0, 0.0)
+
+    for st in (0, 1):
+
+        @pl.when(has_prev(st))
+        def _():
+            t_copy(st).wait_recv()
+            pre[st, 0:8, :] = trecv[st, 8:16, 0 : chan + 128].astype(F32)
+            seg_col[st + 2, 0:8, :] = trecv[st, 8:16, chan + 128 : chan + 256].astype(F32)
+
+        @pl.when(jnp.logical_not(has_prev(st)))
+        def _():
+            pre[st, 0:8, :] = jnp.zeros((8, chan + 128), F32)
+            seg_col[st + 2, 0:8, :] = seg_col[st, 0:8, :]
+
+    def convolved(st, cols):
+        total = jnp.zeros((rows, cols.size), F32)
+        for k in range(4):
+            total = total + conv[k : k + 1, cols] * pre[st, 5 + k : 5 + k + rows, cols]
+        return (total * jax.nn.sigmoid(total)).astype(BF16)
+
+    m_copy = pltpu.make_async_remote_copy(
+        maps.at[m], maps.at[m], msem.at[0], msem.at[1], to_mp, MESH
+    )
+    for st in (0, 1):
+        maps[m, st] = convolved(st, pl.ds(chan, 128))
+    m_copy.start()
+
+    step_b(2, 1)
+
+    @pl.loop(0, chan // 128)
+    def _(n):
+        cols = pl.ds(pl.multiple_of(n * 128, 128), 128)
+        for st in (0, 1):
+            xb[st, :, cols] = convolved(st, cols)
+
+    step_a(2, 2)
+    step_b(1, 3)
+    pltpu.make_async_remote_copy(
+        maps.at[1 - m], maps.at[1 - m], msem.at[0], msem.at[1], to_mp, MESH
+    ).wait_recv()
+
+    hrow = lax.broadcasted_iota(jnp.int32, (128, chan), 0)
+    hcol = lax.broadcasted_iota(jnp.int32, (128, chan), 1)
+    width = chan // heads
+    spread = jnp.where(hcol // width == hrow, 1.0, 0.0).astype(BF16)
+
+    def widened(value):
+        return sum(mm(p, spread) for p in parts(value, 2))
+
+    passing = []
+    for st in (0, 1):
+        b_map, c_map = maps[0, st], maps[1, st]
+        scores = lax.dot_general(
+            c_map, b_map, (((1,), (1,)), ((), ())), preferred_element_type=F32
+        )
+        allowed = (strand_cols[st] == strand_rows[st]) & (ci <= ri)
+        smask[st] = jnp.where(allowed, scores, 0.0)
+        weighted = (xb[st].astype(F32) * widened(step[st])).astype(BF16)
+        state[st] = mm(b_map.astype(F32).T.astype(BF16), weighted)
+        before = seg_col[st + 2, 7:8, 0:1]
+        c = cs[st]
+        flow = jnp.exp(c) * jnp.where(strand_cols[st] == before, 1.0, 0.0)
+        inflow[st] = flow
+        passing.append(widened(flow[rows - 8 : rows])[7:8])
+
+    def e_copy(st, n):
+        cols = pl.ds(n * 512, 512)
+        peer = {"seq": s + 1 if st == 0 else s - 1}
+        return pltpu.make_async_remote_copy(
+            eout.at[st, :, cols], ein.at[st, :, cols], esend.at[st, n], erecv.at[st, n], peer, MESH
+        )
+
+    def hop(st, n):
+        cols = slice(n * 512, (n + 1) * 512)
+
+        @pl.when(has_prev(st))
+        def _():
+            e_copy(st, n).wait_recv()
+
+        @pl.when(jnp.logical_not(has_prev(st)))
+        def _():
+            ein[st, :, cols] = jnp.zeros((128, 512), BF16)
+
+        @pl.when(has_next(st))
+        def _():
+            eout[st, :, cols] = (
+                passing[st][:, cols] * ein[st, :, cols].astype(F32) + state[st, :, cols]
+            ).astype(BF16)
+            e_copy(st, n).start()
+
+    chunks = chan // 512
+
+    def first_hops():
+        for n in range(chunks):
+            for st in (0, 1):
+
+                @pl.when(jnp.logical_not(has_prev(st)))
+                def _():
+                    hop_now(st, n)
+
+    def hop_now(st, n):
+        cols = slice(n * 512, (n + 1) * 512)
+        ein[st, :, cols] = jnp.zeros((128, 512), BF16)
+        eout[st, :, cols] = state[st, :, cols].astype(BF16)
+        e_copy(st, n).start()
+
+    first_hops()
+
+    pairs = chan // 128
+    lane = lax.broadcasted_iota(jnp.int32, (rows, 128), 1)
+
+    def intra(i):
+        st, q = i // pairs, i % pairs
+        cols = pl.ds(pl.multiple_of(q * 128, 128), 128)
+        x_pair = xb[st, :, cols]
+        sm = smask[st]
+        c_all = cs[st]
+        got = []
+        for e in (0, 1):
+            h = 2 * q + e
+            c_col = pltpu.roll(c_all, (128 - h) % 128, 1)[:, 0:1]
+            c_row = ct[st, pl.ds(h, 1), :]
+            dt_row = dtt[st, pl.ds(h, 1), :]
+            mixing = sm * jnp.exp(jnp.minimum(c_col - c_row, 0.0)) * dt_row
+            got.append(mm(mixing.astype(BF16), x_pair))
+        mixed[st, :, cols] = jnp.where(lane < width, got[0], got[1])
+
+    def intra_range(lo, hi):
+        @pl.loop(lo, hi)
+        def _(i):
+            intra(i)
+
+    def later_hops(low_strand):
+        for n in range(chunks):
+            for near in (0, 1):
+                st = near if low_strand else 1 - near
+
+                @pl.when(has_prev(st))
+                def _():
+                    hop(st, n)
+
+    intra_range(0, pairs)
+
+    @pl.when(s < S // 2)
+    def _():
+        later_hops(True)
+
+    @pl.when(s >= S // 2)
+    def _():
+        later_hops(False)
+
+    step_a(2, 3)
+    step_b(2, 2)
+    intra_range(pairs, 2 * pairs)
+    step_b(2, 3)
+    step_c(1)
+
+    @pl.loop(0, chan // 256)
+    def _(n):
+        cols = pl.ds(pl.multiple_of(n * 256, 256), 256)
+        got = mm(u[...], wg[:, cols]).astype(BF16)
+        for st in (0, 1):
+            gate[st, :, cols] = got[st * rows : (st + 1) * rows]
+
+    group = GROUP_HEADS * width
+    for st in (0, 1):
+        for n in range(chan // group):
+            cols = slice(n * group, (n + 1) * group)
+            flow = sum(mm(p, spread[:, cols]) for p in parts(inflow[st], 2))
+            value = (
+                mixed[st, :, cols]
+                + flow * mm(maps[1, st], ein[st, :, cols])
+                + skip[:, cols] * xb[st, :, cols].astype(F32)
+            )
+            wide = gate[st, :, cols].astype(F32)
+            value = value * (wide * jax.nn.sigmoid(wide))
+            scale = lax.rsqrt(jnp.mean(value * value, axis=1, keepdims=True) + 1e-05)
+            normed = (value * scale).astype(BF16)
+            if st == 1:
+                normed = mm(flip, normed).astype(BF16)
+            mix[st, :, cols] = normed
+
+    step_c(2)
+    per_half = S // 2
+
+    def columns(t):
+        direct = mm(mix[0], wo[t])
+        turned_part = mm(mix[1], wo[S - 1 - t])
+        count = out_cols // 256
+        flipped = []
+        for i in range(count):
+            at = count - 1 - i
+            flipped.append(
+                sum(mm(p, flip) for p in parts(turned_part[:, at * 256 : (at + 1) * 256], 2))
+            )
+        return direct + jnp.concatenate(flipped, axis=1)
+
+    def o_copy(i):
+        return pltpu.make_async_remote_copy(
+            osend.at[i], orecv.at[i], osem.at[0, i], osem.at[1, i], to_mp, MESH
+        )
+
+    for i in range(per_half):
+        osend[i] = columns((1 - m) * per_half + i).astype(BF16)
+        o_copy(i).start()
+    for i in range(per_half):
+        own = columns(m * per_half + i)
+        o_copy(i).wait_recv()
+        out[:, i * out_cols : (i + 1) * out_cols] = (own + orecv[i].astype(F32)).astype(BF16)
+
+    settle()
+    h_copy.wait_send()
+    m_copy.wait_send()
+    for st in (0, 1):
+
+        @pl.when(has_next(st))
+        def _():
+            t_copy(st).wait_send()
+            for n in range(chunks):
+                e_copy(st, n).wait_send()
+
+    for i in range(per_half):
+        o_copy(i).wait_send()
+
+
+def fused_body(
+    hidden,
+    segment_ids,
+    norm_gain,
+    w_gate,
+    w_value,
+    w_in_out,
+    w_step,
+    step_bias,
+    decay_rate,
+    skip_gain,
+    conv_value,
+    conv_in_out,
+    w_out,
+):
+    S = lax.axis_size("seq")
+    rows, half = hidden.shape[1:]
+    depth, chan = w_value.shape
+    heads = w_step.shape[1]
+    maps_width = w_in_out.shape[1]
+    out_cols = w_out.shape[1]
+    padded = 128 - heads
+    w_small = jnp.concatenate([w_in_out, jnp.pad(w_step, ((0, 0), (0, padded)))], axis=1)
+    bias = jnp.pad(step_bias, (0, padded))[None]
+    rate = jnp.pad(decay_rate, (0, padded))[None]
+    skip = jnp.repeat(skip_gain, chan // heads)[None]
+    conv = jnp.concatenate([conv_value, conv_in_out], axis=1).astype(F32)
+    conv = jnp.pad(conv, ((0, 4), (0, 0)))
+    anywhere = pl.BlockSpec(memory_space=pl.ANY)
+    vmem = pl.BlockSpec(memory_space=pltpu.VMEM)
+    dma = pltpu.SemaphoreType.DMA
+    result = pl.pallas_call(
+        functools.partial(fused_kernel, S, heads),
+        out_shape=jax.ShapeDtypeStruct((rows, half), BF16),
+        in_specs=[anywhere, vmem, vmem] + [anywhere] * 4 + [vmem] * 4,
+        out_specs=vmem,
+        scratch_shapes=[
+            pltpu.VMEM((2, rows, half), BF16),
+            pltpu.VMEM((S * depth, chan + 256), BF16),
+            pltpu.VMEM((S * depth, chan), BF16),
+            pltpu.VMEM((S, chan, out_cols), BF16),
+            pltpu.VMEM((2 * rows, 2 * half), BF16),
+            pltpu.VMEM((2, rows + 8, chan + maps_width), F32),
+            pltpu.VMEM((2, rows, 128), F32),
+            pltpu.VMEM((2, rows, chan), BF16),
+            pltpu.VMEM((2, 16, chan + 256), BF16),
+            pltpu.VMEM((2, 16, chan + 256), BF16),
+            pltpu.VMEM((2, 2, rows, maps_width), BF16),
+            pltpu.VMEM((2, rows, chan), BF16),
+            pltpu.VMEM((2, rows, rows), F32),
+            pltpu.VMEM((2, rows, 128), F32),
+            pltpu.VMEM((2, 128, rows), F32),
+            pltpu.VMEM((2, 128, rows), F32),
+            pltpu.VMEM((4, rows, 128), F32),
+            pltpu.VMEM((2, 128, chan), F32),
+            pltpu.VMEM((2, rows, 128), F32),
+            pltpu.VMEM((2, 128, chan), BF16),
+            pltpu.VMEM((2, 128, chan), BF16),
+            pltpu.VMEM((2, rows, chan), F32),
+            pltpu.VMEM((2, rows, chan), BF16),
+            pltpu.VMEM((S // 2, rows, out_cols), BF16),
+            pltpu.VMEM((S // 2, rows, out_cols), BF16),
+            dma((5,)),
+            dma((2,)),
+            dma((3, 2, S - 1)),
+            dma((3, 2, S - 1)),
+            dma((3, 2, S - 1)),
+            dma((3, 2, S - 1)),
+            dma((3, 2, S - 1, 2)),
+            dma((3, 2, S - 1, 2)),
+            dma((2, 2)),
+            dma((2,)),
+            dma((2, chan // 512)),
+            dma((2, chan // 512)),
+            dma((2, S // 2)),
+        ],
+        compiler_params=pltpu.CompilerParams(
+            collective_id=0, has_side_effects=True, vmem_limit_bytes=56 * 2**20
+        ),
+        name="fused",
+    )(
+        hidden[0],
+        segment_ids,
+        norm_gain[None],
+        w_value,
+        w_small,
+        w_gate,
+        w_out,
+        bias,
+        rate,
+        skip,
+        conv,
+    )
+    return result[None]
+
+
 def solution(mesh):
     placed = (
         P(("groups", "batch"), "seq", "mp"),
@@ -225,8 +872,11 @@
         P(None, "mp"),
         P("mp", "seq"),
     )
+    sizes = mesh.shape
+    fits = sizes["mp"] == 2 and sizes["groups"] == 2 and sizes["batch"] == 2
+    chosen = fused_body if fits and sizes["seq"] == 4 else body
     return jax.shard_map(
-        body,
+        chosen,
         mesh=mesh,
         in_specs=placed,
         out_specs=P(("groups", "batch"), "seq", "mp"),

time: 403 us -> 118 us (0.29)
  waiting for transfers between devices: 191 us -> 0 us
  Pallas kernels: 0 us -> 110 us
  local copies, waits for them, and re-layouts: 64.4 us -> 5.39 us
  blocking collectives: 57.2 us -> 0 us
  matrix products: 28.5 us -> 0 us
  other arithmetic: 28.4 us -> 2.09 us
  starting transfers between devices: 15.6 us -> 0 us
  between operations: 14 us -> 0.02 us
    all_gather x6 -> x0, waiting for transfers between devices: 154 us -> none  [the longest x1 50.7 us: body(): block_cols = lax.all_gather(w_out, 'seq', axis=1, tiled=True)]
    pallas_call x0 -> x1, Pallas kernels: none -> 110 us  [fused_body(): pl.pallas_call(functools.partial(fused_kernel, S, heads), out_shape=jax.S...]
    all_gather x5 -> x0, blocking collectives: 57.2 us -> none  [the longest x2 19.8 us: entering(): lax.all_gather(part.astype(kind), axis)]
    rev x4 -> x0, local copies, waits for them, and re-layouts: 43.3 us -> none  [the longest x1 15 us: body(): normalize(reverse_full)[:, ::-1] * norm_gain]
    reduce_scatter x1 -> x0, waiting for transfers between devices: 30.5 us -> none  [body(): lax.psum_scatter(running, 'mp', scatter_dimension=1, tiled=True)]
    dot_general x10 -> x0, matrix products: 28.5 us -> none  [the longest x4 12.7 us: body(): jnp.dot(both_in, weight, preferred_element_type=jnp.float32)]
    ppermute x6 -> x0, starting transfers between devices: 15.3 us -> none  [the longest x4 8.64 us: passed_along(): return lax.ppermute(value, axis, pairs)]
    mul x3 -> x0, local copies, waits for them, and re-layouts: 9.94 us -> none  [the longest x2 5.85 us: body(): grouped * lax.rsqrt(jnp.mean(grouped * grouped, axis=3, keepdims=True) +...]
  transfers between devices with their start and end apart: 13 -> 0, of which waited for: 7 -> 0; matrix products, arithmetic and copies ran while one was open for 23% -> 0% of each run, Pallas kernels for 0% -> 0%
where the time goes in v1:
time: 118 us; the launch traced here: 117 us
  Pallas kernels  110 us (93%)
  local copies, waits for them, and re-layouts  5.39 us (5%)
  other arithmetic  2.09 us (2%)
    pallas_call x1, Pallas kernels, fused_body(): pl.pallas_call(functools.partial(fused_kernel, S, heads), out_shape=jax.S...  110 us
    unnamed x4, local copies, waits for them, and re-layouts  2.71 us

profile of v1, /device:TPU:0, one launch (start us, length us, event | category | flops | bytes accessed | tf_op | source)
XLA Modules:
  0.0 117.4 jit_solution(14764073755259062957)
XLA Ops:
  0.0 0.0 copy-start
  0.0 1.3 %pad_bitcast_fusion = (f32[1,128]{1,0:T(1,128)}, f32[1,128]{1,0:T(1,128)}) fusion(f32[16]{0:T(128)} %param.21, f32[16]{0:T(128)} %param.20), kind=kLoop, calls=%fused_computation.8 | loop fusion | bytes 1152 | tf_op jit(solution)/shard_map/broadcast_in_dim | solution.py:787
  1.3 0.7 broadcast_in_dim.18
  2.0 0.7 broadcast_in_dim_reshape.3.skip
  2.7 1.3 %fusion.5.conv = f32[8,1152]{1,0:T(8,128)} fusion(bf16[4,128]{1,0:T(4,128)(2,1)} %param.24, bf16[4,1024]{1,0:T(4,128)(2,1)} %param.23), kind=kLoop, calls=%fused_computation.7 | loop fusion | flops 64512 | bytes 46080 | tf_op jit(solution)/shard_map/jit(_pad)/pad | solution.py:790
  4.0 0.8 copy.14
  4.9 0.0 copy-done
  4.9 0.8 fusion.1.w_small
  5.6 109.9 %fused.1 = bf16[256,1024]{1,0:T(8,128)(2,1)} custom-call(bf16[256,1024]{1,0:T(8,128)(2,1)} %bitcast.8, s32[1,256]{1,0:T(1,128)} %segs.1, f32[1,2048]{1,0:T(1,128)} %bitcast.9, bf16[512,1024]{1,0:T(8,128)(2,1)} %w_value.1, bf16[512,256]{1,0:T(8,128)(2,1)} %fusion.1.w_small, bf16[512,1024]{1,0:T(8,128)(2,1)} %w_gate.1, bf16[1024,512]{1,0:T(8,128)(2,1)} %w_out.1, ...), custom_call_target="tpu_custom_call" | custom-call | tf_op jit(solution)/shard_map/fused/pallas_call | solution.py:794
  115.5 1.9 %copy.16 = bf16[1,256,1024]{2,1,0:T(8,128)(2,1)} copy(bf16[1,256,1024]{2,1,0:T(8,128)(2,1)} %bitcast.7) | data formatting | bytes 1048576
Async XLA Ops:
  0.0 4.9 %copy-start = (bf16[512,128]{1,0:T(8,128)(2,1)S(1)}, bf16[512,128]{1,0:T(8,128)(2,1)}, u32[]{:S(2)}) copy-start(bf16[512,128]{1,0:T(8,128)(2,1)} %param.18) | copy-start | bytes 393220

commit v2 on v1

--- a/solution.py
+++ b/solution.py
@@ -239,13 +239,15 @@
     segs,
     gain,
     w_value,
-    w_small,
+    w_in_out,
     w_gate,
     w_out,
-    bias,
-    rate,
-    skip,
-    conv,
+    step_rows,
+    bias_in,
+    rate_in,
+    skip_in,
+    conv_value,
+    conv_maps,
     out,
     hbuf,
     wv,
@@ -272,6 +274,8 @@
     mix,
     osend,
     orecv,
+    conv,
+    skip,
     lsem,
     hsem,
     zsend,
@@ -314,20 +318,30 @@
     local = [
         pltpu.make_async_copy(hidden, hbuf.at[m], lsem.at[0]),
         pltpu.make_async_copy(w_value, wv.at[own_rows, pl.ds(0, chan)], lsem.at[1]),
-        pltpu.make_async_copy(w_small, wv.at[own_rows, pl.ds(chan, 256)], lsem.at[2]),
+        pltpu.make_async_copy(w_in_out, wv.at[own_rows, pl.ds(chan, 128)], lsem.at[2]),
         pltpu.make_async_copy(w_gate, wg.at[own_rows], lsem.at[3]),
         pltpu.make_async_copy(w_out, wo.at[s], lsem.at[4]),
     ]
     for copy in local:
         copy.start()
+    padding = jnp.zeros((128 - heads, depth), F32)
+    step_all = jnp.concatenate([step_rows[...].astype(F32), padding], axis=0)
+    wv[own_rows, chan + 128 : chan + 256] = step_all.T.astype(BF16)
+
+    def lanes(ref):
+        return jnp.concatenate([ref[...], jnp.zeros((1, 128 - heads), F32)], axis=1)
+
+    conv[0:4, 0:chan] = conv_value[...].astype(F32)
+    conv[0:4, chan : chan + 128] = conv_maps[...].astype(F32)
 
     lone = jnp.where((s == 0) | (s == S - 1), 1, 0)
     pl.semaphore_wait(barrier, 5 - lone)
 
     def piece(w, t, quarter):
-        if w == 2:
-            size = w_out.shape[0] // 4
-            return wo.at[t, pl.ds(pl.multiple_of(quarter * size, size), size)]
+        if w >= 2:
+            size = w_out.shape[0] // 8
+            start = ((w - 2) * 4 + quarter) * size
+            return wo.at[t, pl.ds(pl.multiple_of(start, size), size)]
         size = depth // 4
         start = pl.multiple_of(t * depth + quarter * size, size)
         return (wv, wg)[w].at[pl.ds(start, size)]
@@ -398,10 +412,10 @@
                 y_copy(w, d, k, across).wait_recv()
                 c_copy(w, d, k, 1, across).start()
 
-    def step_c(w):
+    def step_c(w, rounds=range(1, S)):
         other = g * 2 + 1 - b
         other_across = (1 - g) * 2 + 1 - b
-        for k in range(1, S):
+        for k in rounds:
             for d in (0, 1):
 
                 @pl.when(comes(d, k))
@@ -410,7 +424,7 @@
                     c_copy(w, d, k, 1, other_across).wait_recv()
 
     def settle():
-        for w in range(3):
+        for w in range(4):
             for k in range(1, S):
                 for d in (0, 1):
 
@@ -457,6 +471,7 @@
 
     step_a(0, 1)
     step_a(1, 1)
+    start_round(2, 1)
     step_b(0, 1)
     pltpu.make_async_remote_copy(
         hbuf.at[1 - m], hbuf.at[1 - m], hsem.at[0], hsem.at[1], to_mp, MESH
@@ -481,9 +496,10 @@
     step_a(0, 2)
     step_b(1, 1)
     step_a(1, 2)
+    start_round(3, 1)
     step_b(0, 2)
     step_a(0, 3)
-    start_round(2, 1)
+    step_a(2, 1)
     step_b(1, 2)
     step_b(0, 3)
     step_c(0)
@@ -522,12 +538,13 @@
         def _():
             t_copy(st).start()
 
-    step_a(2, 1)
     step_a(1, 3)
+    step_a(3, 1)
+    bias, rate = lanes(bias_in), lanes(rate_in)
     for st in (0, 1):
-        raw = step[st] + bias[...]
+        raw = step[st] + bias
         dt = jnp.maximum(raw, 0.0) + jnp.log1p(jnp.exp(-jnp.abs(raw)))
-        decay = -dt * rate[...]
+        decay = -dt * rate
         c = sum(mm(lower, p) for p in parts(decay, 3))
         cs[st] = c
         ct[st] = c.T
@@ -563,6 +580,7 @@
     m_copy.start()
 
     step_b(2, 1)
+    step_a(2, 2)
 
     @pl.loop(0, chan // 128)
     def _(n):
@@ -570,8 +588,9 @@
         for st in (0, 1):
             xb[st, :, cols] = convolved(st, cols)
 
-    step_a(2, 2)
     step_b(1, 3)
+    step_b(3, 1)
+    step_a(3, 2)
     pltpu.make_async_remote_copy(
         maps.at[1 - m], maps.at[1 - m], msem.at[0], msem.at[1], to_mp, MESH
     ).wait_recv()
@@ -584,6 +603,7 @@
     def widened(value):
         return sum(mm(p, spread) for p in parts(value, 2))
 
+    skip[...] = sum(mm(p, spread) for p in parts(lanes(skip_in), 3))
     passing = []
     for st in (0, 1):
         b_map, c_map = maps[0, st], maps[1, st]
@@ -677,6 +697,8 @@
                     hop(st, n)
 
     intra_range(0, pairs)
+    step_b(2, 2)
+    step_a(2, 3)
 
     @pl.when(s < S // 2)
     def _():
@@ -686,10 +708,9 @@
     def _():
         later_hops(False)
 
-    step_a(2, 3)
-    step_b(2, 2)
+    step_b(3, 2)
+    step_a(3, 3)
     intra_range(pairs, 2 * pairs)
-    step_b(2, 3)
     step_c(1)
 
     @pl.loop(0, chan // 256)
@@ -717,7 +738,7 @@
                 normed = mm(flip, normed).astype(BF16)
             mix[st, :, cols] = normed
 
-    step_c(2)
+    step_b(2, 3)
     per_half = S // 2
 
     def columns(t):
@@ -737,13 +758,25 @@
             osend.at[i], orecv.at[i], osem.at[0, i], osem.at[1, i], to_mp, MESH
         )
 
-    for i in range(per_half):
-        osend[i] = columns((1 - m) * per_half + i).astype(BF16)
-        o_copy(i).start()
-    for i in range(per_half):
-        own = columns(m * per_half + i)
-        o_copy(i).wait_recv()
-        out[:, i * out_cols : (i + 1) * out_cols] = (own + orecv[i].astype(F32)).astype(BF16)
+    def place(h, order):
+        return (1 - h) if order == 0 else h
+
+    for order in (0, 1):
+        rounds = range(1, S - 1) if order == 0 else range(S - 1, S)
+        if order == 1:
+            step_b(3, 3)
+        step_c(2, rounds)
+        step_c(3, rounds)
+        there = (1 - m) * per_half + place(1 - m, order)
+        here = place(m, order)
+        osend[order] = columns(there).astype(BF16)
+        o_copy(order).start()
+        mixed[order, :, 0:out_cols] = columns(m * per_half + here)
+    for order in (0, 1):
+        at = pl.ds(pl.multiple_of(place(m, order) * out_cols, out_cols), out_cols)
+        o_copy(order).wait_recv()
+        own = mixed[order, :, 0:out_cols]
+        out[:, at] = (own + orecv[order].astype(F32)).astype(BF16)
 
     settle()
     h_copy.wait_send()
@@ -781,20 +814,13 @@
     heads = w_step.shape[1]
     maps_width = w_in_out.shape[1]
     out_cols = w_out.shape[1]
-    padded = 128 - heads
-    w_small = jnp.concatenate([w_in_out, jnp.pad(w_step, ((0, 0), (0, padded)))], axis=1)
-    bias = jnp.pad(step_bias, (0, padded))[None]
-    rate = jnp.pad(decay_rate, (0, padded))[None]
-    skip = jnp.repeat(skip_gain, chan // heads)[None]
-    conv = jnp.concatenate([conv_value, conv_in_out], axis=1).astype(F32)
-    conv = jnp.pad(conv, ((0, 4), (0, 0)))
     anywhere = pl.BlockSpec(memory_space=pl.ANY)
     vmem = pl.BlockSpec(memory_space=pltpu.VMEM)
     dma = pltpu.SemaphoreType.DMA
     result = pl.pallas_call(
         functools.partial(fused_kernel, S, heads),
         out_shape=jax.ShapeDtypeStruct((rows, half), BF16),
-        in_specs=[anywhere, vmem, vmem] + [anywhere] * 4 + [vmem] * 4,
+        in_specs=[anywhere, vmem, vmem] + [anywhere] * 4 + [vmem] * 6,
         out_specs=vmem,
         scratch_shapes=[
             pltpu.VMEM((2, rows, half), BF16),
@@ -822,14 +848,16 @@
             pltpu.VMEM((2, rows, chan), BF16),
             pltpu.VMEM((S // 2, rows, out_cols), BF16),
             pltpu.VMEM((S // 2, rows, out_cols), BF16),
+            pltpu.VMEM((8, chan + maps_width), F32),
+            pltpu.VMEM((1, chan), F32),
             dma((5,)),
             dma((2,)),
-            dma((3, 2, S - 1)),
-            dma((3, 2, S - 1)),
-            dma((3, 2, S - 1)),
-            dma((3, 2, S - 1)),
-            dma((3, 2, S - 1, 2)),
-            dma((3, 2, S - 1, 2)),
+            dma((4, 2, S - 1)),
+            dma((4, 2, S - 1)),
+            dma((4, 2, S - 1)),
+            dma((4, 2, S - 1)),
+            dma((4, 2, S - 1, 2)),
+            dma((4, 2, S - 1, 2)),
             dma((2, 2)),
             dma((2,)),
             dma((2, chan // 512)),
@@ -845,13 +873,15 @@
         segment_ids,
         norm_gain[None],
         w_value,
-        w_small,
+        w_in_out,
         w_gate,
         w_out,
-        bias,
-        rate,
-        skip,
-        conv,
+        w_step.T,
+        step_bias[None],
+        decay_rate[None],
+        skip_gain[None],
+        conv_value,
+        conv_in_out,
     )
     return result[None]
 

time: 118 us -> 112 us (0.949)
  local copies, waits for them, and re-layouts: 5.39 us -> 1.87 us
  other arithmetic: 2.09 us -> 0 us
    broadcast_in_dim x2 -> x0, local copies, waits for them, and re-layouts: 2.01 us -> none  [the longest x1 1.29 us: fused_body(): rate = jnp.pad(decay_rate, (0, padded))[None]]
    pad x1 -> x0, other arithmetic: 1.34 us -> none  [fused_body(): conv = jnp.pad(conv, ((0, 4), (0, 0)))]
    unnamed x4 -> x1, local copies, waits for them, and re-layouts: 2.71 us -> 1.87 us
where the time goes in v2:
time: 112 us
  Pallas kernels  110 us (98%)
  local copies, waits for them, and re-layouts  1.87 us (2%)
    pallas_call x1, Pallas kernels, fused_body(): pl.pallas_call(functools.partial(fused_kernel, S, heads), out_shape=jax.S...  110 us

profile of v2, /device:TPU:0, one launch (start us, length us, event | category | flops | bytes accessed | tf_op | source)
XLA Modules:
  0.0 111.7 jit_solution(595921032621985993)
XLA Ops:
  0.0 109.8 %fused.1 = bf16[256,1024]{1,0:T(8,128)(2,1)} custom-call(bf16[256,1024]{1,0:T(8,128)(2,1)} %bitcast.8, s32[1,256]{1,0:T(1,128)} %segs.1, f32[1,2048]{1,0:T(1,128)} %bitcast.10, bf16[512,1024]{1,0:T(8,128)(2,1)} %w_value.1, bf16[512,128]{1,0:T(8,128)(2,1)} %w_in_out.1, bf16[512,1024]{1,0:T(8,128)(2,1)} %w_gate.1, bf16[1024,512]{1,0:T(8,128)(2,1)} %w_out.1, ...), custom_call_target="tpu_custom_call" | custom-call | tf_op jit(solution)/shard_map/fused/pallas_call | solution.py:820
  109.8 1.9 %copy.15 = bf16[1,256,1024]{2,1,0:T(8,128)(2,1)} copy(bf16[1,256,1024]{2,1,0:T(8,128)(2,1)} %bitcast.7) | data formatting | bytes 1048576
